TPU v7x, 32 devices: a whole 2x2x4 slice. The times are simulated.
32 devices in a mesh: groups: 2 (over y), queue: 4 (over z), dp: 4 (over x, core).
Axes of the slice: x: 2, y: 2, z: 4, core: 2. Of those that a mesh axis runs over, the one named last changes fastest.
Arguments:
- query_inputs: bfloat16 [8192, 1024], P(('groups', 'queue', 'dp')), parts along dimension 0, may hold values from -30 to 30
- key_inputs: bfloat16 [512, 1024], P(('groups', 'queue', 'dp')), parts along dimension 0, may hold values from -6 to 6
- query_weight: bfloat16 [1024, 1024], replicated, may hold values from -4 to 4
- key_weight: bfloat16 [1024, 1024], replicated, may hold values from -0.1875 to 0.1875
- queue_keys: bfloat16 [2048, 1024], P(('groups', 'queue')), parts along dimension 0, may hold values from -2 to 2
- write_pointer: int32 [2], P('groups'), parts along dimension 0, may hold values from 0 to 255
- slot_owner: int32 [32], P('groups'), parts along dimension 0, may hold values from 0 to 15, each once
- positive_index: int32 [8192], P(('groups', 'queue', 'dp')), parts along dimension 0, may hold values from 0 to 1023
Outputs:
- loss: float32 [8192], P(('groups', 'queue', 'dp')), parts along dimension 0
- query_weight_grad: float32 [2048, 1024], P(('groups', 'queue', 'dp')), parts along dimension 0
- new_queue: bfloat16 [2048, 1024], P(('groups', 'queue')), parts along dimension 0
There are 2 independent parts, one for each index of `groups`. A program takes and returns all parts, laid end to end along the dimension named above; an argument that names none is the same for every part. Nothing has to cross between parts.
Inputs may be any that keep to these rules, and one draw needn't show every extreme that they name: slot_owner is a permutation of 0 to 15.
All inputs are finite; a program needn't handle non-finite values.
Results may differ from a plain program's by a relative error of at most 0.0075.
Values may be sent and summed in bfloat16 or wider, within the bound.
A program may use at most 192 MiB of HBM per device.

v0:
```python
import jax
import jax.numpy as jnp
from jax import lax
from jax.sharding import PartitionSpec as P

temper = 0.05


def make_fold(units, mapped):

    def fold(carry, piece, start):
        top, total, mixture, chosen = carry
        scores = (
            lax.dot_general(
                units, piece, (((1,), (1,)), ((), ())), preferred_element_type=jnp.float32
            )
            / temper
        )
        new_top = jnp.maximum(top, jnp.max(scores, -1))
        expo = jnp.exp(scores - new_top[:, None])
        total = jnp.sum(expo, -1)
        mixture = jnp.dot(expo.astype(jnp.bfloat16), piece, preferred_element_type=jnp.float32)
        count = piece.shape[0]
        hit = (mapped >= 0) & (mapped < count)
        picked = jnp.take(piece, jnp.clip(mapped, 0, count - 1), axis=0).astype(jnp.float32)
        chosen = jnp.where(hit[:, None], picked, 0.0)
        return (new_top, total, mixture, chosen)

    return fold


def start_carry(count, width):
    return (
        jnp.full((count,), -1e30, jnp.float32),
        jnp.zeros((count,), jnp.float32),
        jnp.zeros((count, width), jnp.float32),
        jnp.zeros((count, width), jnp.float32),
    )


def body(
    query_inputs,
    key_inputs,
    query_weight,
    key_weight,
    queue_keys,
    write_pointer,
    slot_owner,
    positive_index,
):
    q_dev, width = query_inputs.shape
    k_dev = queue_keys.shape[0]
    new_dev = key_inputs.shape[0]
    n_dp = lax.axis_size("dp")
    query = jnp.dot(query_inputs, query_weight, preferred_element_type=jnp.float32)
    inv_len = lax.rsqrt(jnp.sum(query * query, -1, keepdims=True) + 1e-06)
    unit_f = query * inv_len
    unit = unit_f.astype(jnp.bfloat16)
    fold = make_fold(unit, positive_index)
    top, total, mixture, chosen = fold(
        start_carry(q_dev, width),
        lax.all_gather(queue_keys, "queue", axis=0, tiled=True),
        jnp.int32(0),
    )
    mixture = mixture / total[:, None]
    positive = jnp.sum(unit.astype(jnp.float32) * chosen, -1) / temper
    loss = top + jnp.log(total) - positive
    grad_unit = (mixture - chosen) / temper
    grad_query = (
        (grad_unit - unit_f * jnp.sum(unit_f * grad_unit, -1, keepdims=True)) * inv_len
    ).astype(jnp.bfloat16)
    n_all = lax.axis_size(("queue", "dp"))
    share = width // n_all
    term = lax.dot_general(
        query_inputs, grad_query, (((0,), (0,)), ((), ())), preferred_element_type=jnp.float32
    )
    summed = lax.psum(term, ("queue", "dp"))
    grad_rows = lax.dynamic_slice_in_dim(summed, lax.axis_index(("queue", "dp")) * share, share, 0)
    fresh = jnp.dot(key_inputs, key_weight, preferred_element_type=jnp.float32)
    fresh = (fresh * lax.rsqrt(jnp.sum(fresh * fresh, -1, keepdims=True) + 1e-06)).astype(
        jnp.bfloat16
    )
    arrived = lax.all_gather(fresh, ("queue", "dp"), axis=0, tiled=True)
    n_blocks = slot_owner.shape[0]
    slots_here = lax.axis_index("queue") * n_dp + jnp.arange(n_dp, dtype=jnp.int32)
    match = slot_owner[None, :] == slots_here[:, None]
    owner_block = jnp.sum(jnp.where(match, jnp.arange(n_blocks, dtype=jnp.int32)[None, :], 0), -1)
    offset = (jnp.arange(k_dev, dtype=jnp.int32) - write_pointer[0]) % k_dev
    live = offset < n_dp * new_dev
    sub_block = jnp.minimum(offset // new_dev, n_dp - 1)
    source = jnp.take(owner_block, sub_block) * new_dev + offset % new_dev
    new_queue = jnp.where(live[:, None], jnp.take(arrived, source, axis=0), queue_keys)
    return (loss, grad_rows, new_queue)


def solution(mesh):
    in_specs = (
        P(("groups", "queue", "dp"), None),
        P(("groups", "queue", "dp"), None),
        P(),
        P(),
        P(("groups", "queue"), None),
        P("groups"),
        P("groups"),
        P(("groups", "queue", "dp")),
    )
    out_specs = (
        P(("groups", "queue", "dp")),
        P(("groups", "queue", "dp"), None),
        P(("groups", "queue"), None),
    )
    return jax.shard_map(body, mesh=mesh, in_specs=in_specs, out_specs=out_specs, check_vma=False)
```

profile of v0, /device:TPU:0, one launch (start us, length us, event | category | flops | bytes accessed | tf_op | source)
XLA Modules:
  0.0 193.7 jit_solution(15796007540766359770)
XLA Ops:
  7.2 0.0 copy-start
  7.2 0.0 all-gather.2.cloned.1.call-start
  7.2 0.7 all-gather.2.cloned.1.call-update
  7.9 0.0 all-reduce.2.cloned.1.call-start
  8.6 0.7 compare_select_fusion.9
  9.3 0.7 compare_and_fusion.1
  10.0 0.0 copy-done
  10.0 1.8 multiply_reduce_fusion.2
  11.9 46.4 %all-gather.2.cloned.1.call-done = bf16[1024,1024]{1,0:T(8,128)(2,1)} async-done(((bf16[256,1024]{1,0:T(8,128)(2,1)}), bf16[1024,1024]{1,0:T(8,128)(2,1)}) %all-gather.2.cloned.1.call-update) | async-done | bytes 2097168 | tf_op jit(solution)/shard_map/all_gather | solution.py:62
  58.3 2.4 %fusion.14 = (f32[256]{0:T(256)S(1)}, f32[256,1024]{1,0:T(8,128)S(1)}) fusion(bf16[1024,1024]{1,0:T(8,128)(2,1)} %all-gather.2.cloned.1.call-done, f32[256,1024]{1,0:T(8,128)S(1)} %get-tuple-element.23, f32[256]{0:T(256)S(1)} %add_rsqrt_fusion), kind=kOutput, calls=%fused_computation.68 | convolution fusion | flops 537919232 | bytes 4196352 | tf_op jit(solution)/shard_map/dot_general | solution.py:14
  60.7 0.0 copy-start.1
  60.7 1.0 copy-done.1
  61.7 0.3 fusion.3
  62.0 4.2 %gather_fusion = bf16[256,1024]{1,0:T(8,128)(2,1)} fusion(bf16[1024,1024]{1,0:T(8,128)(2,1)} %all-gather.2.cloned.1.call-done, s32[1024]{0:T(1024)S(1)} %pad_clamp_fusion.1), kind=kCustom, calls=%fused_computation | custom fusion | bytes 1049600 | tf_op jit(solution)/shard_map/jit(_take)/gather | solution.py:25
  66.2 0.0 copy-start.2
  66.2 3.1 %multiply_reduce_fusion = (f32[256]{0:T(256)S(1)}, f32[256]{0:T(256)S(1)}, f32[256,1024]{1,0:T(8,128)S(1)}) fusion(f32[256,1024]{1,0:T(8,128)S(1)} %get-tuple-element.23, f32[256]{0:T(256)S(1)} %add_rsqrt_fusion, bf16[256,1024]{1,0:T(8,128)(2,1)} %gather_fusion, pred[256]{0:T(512)(128)(4,1)S(1)} %get-tuple-element.16, ...), kind=kOutput, calls=%fused_computation.8 | convolution fusion | flops 540802560 | bytes 5772800 | tf_op jit(solution)/shard_map/dot_general | solution.py:22
  69.3 0.0 copy-done.2
  69.3 3.0 %convolution_bitcast_fusion = f32[1024,1024]{0,1:T(8,128)} fusion(bf16[256,1024]{1,0:T(8,128)(2,1)S(1)} %copy-done.2, f32[256,1024]{1,0:T(8,128)S(1)} %get-tuple-element.26, f32[256,1024]{1,0:T(8,128)S(1)} %get-tuple-element.23, f32[256]{0:T(256)S(1)} %get-tuple-element.12, f32[256]{0:T(256)S(1)} %add_rsqrt_fusion), kind=kOutput, calls=%fused_computation.2 | convolution fusion | flops 538181632 | bytes 6817792 | tf_op jit(solution)/shard_map/dot_general | solution.py:74
  72.3 0.0 copy-start.4
  72.3 0.0 copy-start.3
  72.3 0.0 all-reduce.2.cloned.1.call-update
  72.3 0.6 copy-done.4
  72.9 0.2 select_reduce_fusion
  73.1 0.6 fusion.13
  73.7 2.5 %compare_select_fusion = (s32[256,1]{0,1:T(1,128)S(1)}, s32[256,1]{0,1:T(1,128)S(1)}) fusion(s32[]{:T(128)} %bitcast.16, s32[]{:T(128)} %bitcast.5, s32[]{:T(128)} %bitcast.4, s32[]{:T(128)} %bitcast.3, s32[]{:T(128)} %bitcast.2), kind=kLoop, calls=%fused_computation.23 | loop fusion | flops 12800 | bytes 2068 | tf_op jit(solution)/shard_map/jit(_take)/jit(_where)/select_n | solution.py:92
  76.2 0.0 copy-done.3
  76.3 2.2 %multiply_reduce_fusion.3 = (f32[16]{0:T(128)S(1)}, f32[16,1024]{1,0:T(8,128)S(1)}) fusion(bf16[16,1024]{1,0:T(8,128)(2,1)S(1)} %copy-done.3, bf16[1024,1024]{1,0:T(8,128)(2,1)} %param.11), kind=kOutput, calls=%fused_computation.22 | convolution fusion | flops 33587184 | bytes 2195520 | tf_op jit(solution)/shard_map/dot_general | solution.py:79
  78.5 0.1 multiply_convert_fusion.3
  78.5 23.4 %all_gather.7 = bf16[256,1024]{1,0:T(8,128)(2,1)S(1)} all-gather(bf16[16,1024]{1,0:T(8,128)(2,1)S(1)} %multiply_convert_fusion.3), channel_id=1, replica_groups=mesh['groups'=2,'queue'=4,'dp'=4] {'queue','dp'}, dimensions={0}, use_global_device_ids=true | all-gather | bytes 557056 | tf_op jit(solution)/shard_map/all_gather | solution.py:83
  101.9 1.2 gather_fusion.1
  103.1 2.0 %select_select_fusion = bf16[256,1024]{1,0:T(8,128)(2,1)} fusion(bf16[256,1024]{1,0:T(8,128)(2,1)} %param.12, bf16[256,1024]{1,0:T(8,128)(2,1)S(1)} %gather_fusion.1, pred[256]{0:T(512)(128)(4,1)S(1)} %get-tuple-element.29, pred[256]{0:T(512)(128)(4,1)S(1)} %get-tuple-element.30), kind=kLoop, calls=%fused_computation.16 | loop fusion | flops 524288 | bytes 1573376 | tf_op jit(solution)/shard_map/jit(_where)/select_n | solution.py:92
  105.1 0.6 multiply_subtract_fusion
  105.7 79.1 %all-reduce.2.cloned.1.call-done = f32[1024,1024]{0,1:T(8,128)} async-done(((f32[1024,1024]{0,1:T(8,128)}), f32[1024,1024]{0,1:T(8,128)}) %all-reduce.2.cloned.1.call-update) | async-done | bytes 4194320 | tf_op jit(solution)/shard_map/psum | solution.py:77
  184.8 1.2 constant_dynamic-slice_fusion
  186.0 0.9 copy.13
  (7 shorter events, 0.1 us)
Async XLA Ops:
  7.2 2.8 %copy-start = (bf16[1024,1024]{1,0:T(8,128)(2,1)S(1)}, bf16[1024,1024]{1,0:T(8,128)(2,1)}, u32[]{:S(2)}) copy-start(bf16[1024,1024]{1,0:T(8,128)(2,1)} %param.10) | copy-start | bytes 6291460
  7.2 51.1 %all-gather.2.cloned.1.call-start = ((), (), s32[]{:S(2)}) async-start(), calls=%async_computation | async-start | bytes 2621440 | tf_op jit(solution)/shard_map/all_gather | solution.py:62
  7.9 176.9 %all-reduce.2.cloned.1.call-start = ((), (), s32[]{:S(2)}) async-start(), calls=%async_computation.1 | async-start | bytes 8388608 | tf_op jit(solution)/shard_map/psum | solution.py:77
  60.7 1.0 copy-start.1
  66.2 3.1 %copy-start.2 = (bf16[256,1024]{1,0:T(8,128)(2,1)S(1)}, bf16[256,1024]{1,0:T(8,128)(2,1)}, u32[]{:S(2)}) copy-start(bf16[256,1024]{1,0:T(8,128)(2,1)} %param.8) | copy-start | bytes 1572868
  72.3 0.7 copy-start.4
  72.3 4.0 %copy-start.3 = (bf16[16,1024]{1,0:T(8,128)(2,1)S(1)}, bf16[16,1024]{1,0:T(8,128)(2,1)}, u32[]{:S(2)}) copy-start(bf16[16,1024]{1,0:T(8,128)(2,1)} %param.9) | copy-start | bytes 98308
Sparse Core Ops, SparseCore 0:
  9.6 48.6 all-gather.1
  72.4 112.3 all-reduce.1
where the time goes:
time: 194 us
  waiting for transfers between devices  126 us (65%)
  blocking collectives  23.4 us (12%)
  between operations  14.8 us (8%)
  matrix products  12.5 us (6%)
  local copies, waits for them, and re-layouts  9.73 us (5%)
  other arithmetic  7.08 us (4%)
    psum x1, waiting for transfers between devices, body(): summed = lax.psum(term, ('queue', 'dp'))  79.1 us
    all_gather x1, waiting for transfers between devices, body(): lax.all_gather(queue_keys, 'queue', axis=0, tiled=True)  46.4 us
    all_gather x1, blocking collectives, body(): arrived = lax.all_gather(fresh, ('queue', 'dp'), axis=0, tiled=True)  23.4 us
    gather x1, local copies, waits for them, and re-layouts, fold(): jnp.take(piece, jnp.clip(mapped, 0, count - 1), axis=0).astype(jnp.float32)  4.21 us
  transfers between devices with their start and end apart: 2, of which 2 were waited for; matrix products, arithmetic and copies ran while one was open for 6% of the time, Pallas kernels for 0%

commit v1 on v0

v1 whole, which is shorter than its diff:
```python
import functools

import jax
import jax.numpy as jnp
from jax import lax
from jax.experimental import pallas as pl
from jax.experimental.pallas import tpu as pltpu
from jax.sharding import PartitionSpec as P

temper = 0.05
MESH = pl.DeviceIdType.MESH
F32 = jnp.float32
BF16 = jnp.bfloat16


def dot(a, b, da, db):
    return lax.dot_general(a, b, (((da,), (db,)), ((), ())), preferred_element_type=F32)


def kernel(
    nq, nd,
    pointer_ref, owner_ref, index_ref, x_hbm, kin_hbm, wq_hbm, wk_hbm, keys_hbm,
    loss_ref, grad_ref, queue_ref,
    x_ref, kin_ref, wq_ref, wk_ref, keys, fresh,
    unit_f, unit, inv_len, top, total, posit, pos_col, mixture, chosen,
    xt, grad_q, core_out, core_in, part, x_out, x_in, up_in, down_in, z_out,
    load_sem, up_send, down_send, z_recv, x_send, x_recv, c_send, c_recv,
    fz_send, fz_recv, f_send, f_recv,
    gc_send, gc_recv, gx_send, gx_recv, gu_send, gd_send, gu_recv, gd_recv,
):
    q = lax.axis_index("queue")
    d = lax.axis_index("dp")
    hi, lo = d // 2, d % 2
    side = (1 - hi) * 2 + lo
    mate = hi * 2 + (1 - lo)
    cross = (1 - hi) * 2 + (1 - lo)
    rows, width = x_ref.shape
    n_keys = keys.shape[1]
    quarter = n_keys // nd
    new = kin_ref.shape[0]
    share = grad_ref.shape[0]

    loads = [
        pltpu.make_async_copy(src, dst, load_sem.at[i])
        for i, (src, dst) in enumerate(
            (
                (x_hbm, x_ref),
                (wq_hbm, wq_ref),
                (keys_hbm, keys.at[q]),
                (kin_hbm, kin_ref),
                (wk_hbm, wk_ref),
            )
        )
    ]
    for load in loads:
        load.start()

    def piece(r, part_of):
        return keys.at[r, pl.ds(pl.multiple_of(part_of * quarter, quarter), quarter)]

    def remote(src, dst, send, recv, where):
        return pltpu.make_async_remote_copy(
            src_ref=src, dst_ref=dst, send_sem=send, recv_sem=recv,
            device_id=where, device_id_type=MESH,
        )

    own_piece = keys_hbm.at[pl.ds(pl.multiple_of(d * quarter, quarter), quarter)]

    def key_up(r, src=None):
        src = piece(r, d) if src is None else src
        return remote(src, piece(r, d), up_send.at[r], z_recv.at[r], {"queue": jnp.minimum(q + 1, nq - 1)})

    def key_down(r, src=None):
        src = piece(r, d) if src is None else src
        return remote(src, piece(r, d), down_send.at[r], z_recv.at[r], {"queue": jnp.maximum(q - 1, 0)})

    def key_side(r):
        return remote(piece(r, d), piece(r, d), x_send.at[r], x_recv.at[r], {"dp": side})

    def key_side_in(r):
        return remote(piece(r, side), piece(r, side), x_send.at[r], x_recv.at[r], {"dp": side})

    def key_mate(r, k, part_of):
        return remote(piece(r, part_of), piece(r, part_of), c_send.at[r, k], c_recv.at[r, k], {"dp": mate})

    barrier = pltpu.get_barrier_semaphore()
    pl.semaphore_signal(barrier, inc=1, device_id={"dp": side}, device_id_type=MESH)
    pl.semaphore_signal(barrier, inc=1, device_id={"dp": mate}, device_id_type=MESH)
    for r in range(nq):
        @pl.when(q != r)
        def _():
            pl.semaphore_signal(barrier, inc=1, device_id={"queue": r}, device_id_type=MESH)
    pl.semaphore_wait(barrier, nq + 1)

    @pl.when(q < nq - 1)
    def _():
        key_up(q, own_piece).start()

    @pl.when(q > 0)
    def _():
        key_down(q, own_piece).start()

    loads[0].wait()
    loads[1].wait()
    query = jnp.dot(x_ref[...], wq_ref[...], preferred_element_type=F32)
    scale = lax.rsqrt(jnp.sum(query * query, -1, keepdims=True) + 1e-06)
    inv_len[...] = scale
    query = query * scale
    unit_f[...] = query
    unit[...] = query.astype(BF16)
    top[...] = jnp.full(top.shape, -1e30, F32)
    total[...] = jnp.zeros(total.shape, F32)
    posit[...] = jnp.zeros(posit.shape, F32)
    mixture[...] = jnp.zeros(mixture.shape, F32)
    chosen[...] = jnp.zeros(chosen.shape, F32)
    eye = lax.broadcasted_iota(jnp.int32, (rows, rows), 0) == lax.broadcasted_iota(
        jnp.int32, (rows, rows), 1
    )
    pos_col[...] = jnp.sum(jnp.where(eye, index_ref[...], 0), -1, keepdims=True)

    def fold(r):
        block = keys[r]
        scores = dot(unit[...], block, 1, 1) / temper
        hit = lax.broadcasted_iota(jnp.int32, (rows, n_keys), 1) + r * n_keys == pos_col[...]
        posit[...] += jnp.sum(jnp.where(hit, scores, 0.0), -1, keepdims=True)
        old = top[...]
        high = jnp.maximum(old, jnp.max(scores, -1, keepdims=True))
        decay = jnp.exp(old - high)
        expo = jnp.exp(scores - high)
        top[...] = high
        total[...] = total[...] * decay + jnp.sum(expo, -1, keepdims=True)
        mixture[...] = mixture[...] * decay + jnp.dot(
            expo.astype(BF16), block, preferred_element_type=F32
        )
        chosen[...] += jnp.dot(
            jnp.where(hit, 1.0, 0.0).astype(BF16), block, preferred_element_type=F32
        )

    loads[3].wait()
    loads[4].wait()
    made = jnp.dot(kin_ref[...], wk_ref[...], preferred_element_type=F32)
    made = (made * lax.rsqrt(jnp.sum(made * made, -1, keepdims=True) + 1e-06)).astype(BF16)
    fresh[d, pl.ds(pl.multiple_of(q * new, new), new)] = made

    def fresh_out(r):
        slot = fresh.at[d, pl.ds(pl.multiple_of(q * new, new), new)]
        return remote(slot, slot, fz_send.at[r], fz_recv.at[q], {"queue": r})

    def fresh_in(r):
        slot = fresh.at[d, pl.ds(pl.multiple_of(r * new, new), new)]
        return remote(slot, slot, fz_send.at[r], fz_recv.at[r], {"queue": r})

    def fresh_move(k, part_of, where):
        return remote(fresh.at[part_of], fresh.at[part_of], f_send.at[k], f_recv.at[k], {"dp": where})

    turned = x_ref[...].astype(F32).T
    for p in range(nd):
        xt[p] = jnp.concatenate(
            [turned[(r * nd + p) * share : (r * nd + p + 1) * share] for r in range(nq)], axis=0
        ).astype(BF16)

    loads[2].wait()
    fold(q)

    def others(s, act):
        @pl.when(q - s >= 0)
        def _():
            act(q - s, True)

        @pl.when(q + s <= nq - 1)
        def _():
            act(q + s, False)

    def pass_on(r, upward):
        key_side_in_z = remote(piece(r, d), piece(r, d), up_send.at[r], z_recv.at[r], {"dp": side})
        key_side_in_z.wait_recv()
        if upward:
            @pl.when(q < nq - 1)
            def _():
                key_up(r).start()
        else:
            @pl.when(q > 0)
            def _():
                key_down(r).start()
        key_side(r).start()
        key_mate(r, 0, d).start()

    def pass_side(r, upward):
        key_side_in(r).wait_recv()
        key_mate(r, 1, side).start()

    def take(r, upward):
        key_mate(r, 0, mate).wait_recv()
        key_mate(r, 1, cross).wait_recv()
        fold(r)

    def step(s, carry):
        @pl.when(s <= nq - 1)
        def _():
            others(s, pass_on)

        @pl.when(s == nq - 1)
        def _():
            for r in range(nq):
                @pl.when(q != r)
                def _():
                    fresh_out(r).start()

        @pl.when(s >= 2)
        def _():
            others(s - 1, pass_side)

            def both(k, carry):
                r = q + (s - 1) * (2 * k - 1)

                @pl.when((r >= 0) & (r <= nq - 1))
                def _():
                    take(r, True)

                return carry

            lax.fori_loop(0, 2, both, 0)

        return carry

    lax.fori_loop(1, nq + 1, step, 0)

    for r in range(nq):
        @pl.when(q != r)
        def _():
            fresh_in(r).wait_recv()
    fresh_move(0, d, side).start()
    fresh_move(1, d, mate).start()

    count = total[...]
    loss_col = top[...] + jnp.log(count) - posit[...]
    loss_ref[...] = jnp.sum(jnp.where(eye, loss_col, 0.0), 0, keepdims=True)
    grad_unit = (mixture[...] / count - chosen[...]) / temper
    units = unit_f[...]
    grad_q[...] = (
        (grad_unit - units * jnp.sum(units * grad_unit, -1, keepdims=True)) * inv_len[...]
    ).astype(BF16)

    def term(p):
        return jnp.dot(xt[p], grad_q[...], preferred_element_type=F32)

    def grad_mate(k):
        return remote(core_out.at[k], core_in.at[k], gc_send.at[k], gc_recv.at[k], {"dp": mate})

    def grad_side(r):
        return remote(x_out.at[r], x_in.at[r], gx_send.at[r], gx_recv.at[r], {"dp": side})

    def grad_up(r):
        return remote(z_out.at[r], up_in.at[r], gu_send.at[r], gu_recv.at[r], {"queue": jnp.minimum(q + 1, nq - 1)})

    def grad_down(r):
        return remote(z_out.at[r], down_in.at[r], gd_send.at[r], gd_recv.at[r], {"queue": jnp.maximum(q - 1, 0)})

    core_out[0] = term(cross).reshape(nq, share, width).astype(BF16)
    grad_mate(0).start()
    core_out[1] = term(mate).reshape(nq, share, width).astype(BF16)
    grad_mate(1).start()
    far = term(side).reshape(nq, share, width)
    part[...] = far
    grad_mate(0).wait_recv()
    x_out[...] = (part[...] + core_in[0].astype(F32)).astype(BF16)

    def in_turn(t, act_up, act_down):
        for_up = nq - 1 - (t - q)

        @pl.when((t >= q) & (for_up > q))
        def _():
            act_up(for_up)

        for_down = t - (nq - 1 - q)

        @pl.when((for_down >= 0) & (for_down < q))
        def _():
            act_down(for_down)

    def send_side(t, carry):
        in_turn(t, lambda r: grad_side(r).start(), lambda r: grad_side(r).start())
        return carry

    lax.fori_loop(0, nq - 1, send_side, 0)
    grad_side(q).start()

    part[...] = term(d).reshape(nq, share, width)
    fresh_move(0, side, side).wait_recv()
    fresh_move(2, side, mate).start()
    grad_mate(1).wait_recv()
    part[...] += core_in[1].astype(F32)

    fresh_move(1, mate, mate).wait_recv()
    fresh_move(2, cross, mate).wait_recv()
    n_new = nd * nq * new
    column = lax.broadcasted_iota(jnp.int32, (1, n_new), 1)
    block = (column % (nq * new)) // new * nd + column // (nq * new)
    goes = jnp.zeros((1, n_new), jnp.int32)
    for b in range(nd * nq):
        goes = jnp.where(block == b, owner_ref[b], goes)
    goes = goes * new + column % new - q * (nd * new)
    offset = lax.broadcasted_iota(jnp.int32, (n_keys, 1), 0) - pointer_ref[0]
    offset = jnp.where(offset < 0, offset + n_keys, offset)
    pick = jnp.where((goes == offset) & (offset < nd * new), 1.0, 0.0).astype(BF16)
    moved = jnp.dot(pick, fresh[...].reshape(n_new, width), preferred_element_type=F32)
    queue_ref[...] = jnp.where(offset < nd * new, moved, keys[q].astype(F32)).astype(BF16)

    def up_step(r):
        grad_side(r).wait_recv()
        part[r] += x_in[r].astype(F32)

        @pl.when(q > 0)
        def _():
            grad_up(r).wait_recv()
            part[r] += up_in[r].astype(F32)

        z_out[r] = part[r].astype(BF16)
        grad_up(r).start()

    def down_step(r):
        grad_side(r).wait_recv()
        part[r] += x_in[r].astype(F32)

        @pl.when(q < nq - 1)
        def _():
            grad_down(r).wait_recv()
            part[r] += down_in[r].astype(F32)

        z_out[r] = part[r].astype(BF16)
        grad_down(r).start()

    def chain(t, carry):
        in_turn(t, up_step, down_step)
        return carry

    lax.fori_loop(0, nq - 1, chain, 0)
    grad_side(q).wait_recv()
    part[q] += x_in[q].astype(F32)

    @pl.when(q > 0)
    def _():
        grad_up(q).wait_recv()
        part[q] += up_in[q].astype(F32)

    @pl.when(q < nq - 1)
    def _():
        grad_down(q).wait_recv()
        part[q] += down_in[q].astype(F32)

    grad_ref[...] = part[q]

    def drain(r, carry):
        @pl.when((r <= q) & (q < nq - 1))
        def _():
            key_up(r).wait_send()

        @pl.when((r >= q) & (q > 0))
        def _():
            key_down(r).wait_send()

        @pl.when(r != q)
        def _():
            key_side(r).wait_send()
            key_mate(r, 0, d).wait_send()
            key_mate(r, 1, side).wait_send()
            fresh_out(r).wait_send()

        grad_side(r).wait_send()

        @pl.when(r > q)
        def _():
            grad_up(r).wait_send()

        @pl.when(r < q)
        def _():
            grad_down(r).wait_send()

        return carry

    lax.fori_loop(0, nq, drain, 0)
    fresh_move(0, d, side).wait_send()
    fresh_move(1, d, mate).wait_send()
    fresh_move(2, side, mate).wait_send()
    grad_mate(0).wait_send()
    grad_mate(1).wait_send()


def make_body(nq, nd):

    def body(
        query_inputs, key_inputs, query_weight, key_weight,
        queue_keys, write_pointer, slot_owner, positive_index,
    ):
        rows, width = query_inputs.shape
        n_keys = queue_keys.shape[0]
        new = key_inputs.shape[0]
        share = width // (nq * nd)
        smem = pl.BlockSpec(memory_space=pltpu.SMEM)
        vmem = pl.BlockSpec(memory_space=pltpu.VMEM)
        hbm = pl.BlockSpec(memory_space=pl.ANY)
        V = pltpu.VMEM
        S = pltpu.SemaphoreType.DMA
        loss, grad, queue = pl.pallas_call(
            functools.partial(kernel, nq, nd),
            out_shape=(
                jax.ShapeDtypeStruct((1, rows), F32),
                jax.ShapeDtypeStruct((share, width), F32),
                jax.ShapeDtypeStruct((n_keys, width), BF16),
            ),
            in_specs=[smem, smem, vmem, hbm, hbm, hbm, hbm, hbm],
            out_specs=(vmem, vmem, vmem),
            scratch_shapes=[
                V((rows, width), BF16),
                V((new, width), BF16),
                V(query_weight.shape, BF16),
                V(key_weight.shape, BF16),
                V((nq, n_keys, width), BF16),
                V((nd, nq * new, width), BF16),
                V((rows, width), F32),
                V((rows, width), BF16),
                V((rows, 1), F32),
                V((rows, 1), F32),
                V((rows, 1), F32),
                V((rows, 1), F32),
                V((rows, 1), jnp.int32),
                V((rows, width), F32),
                V((rows, width), F32),
                V((nd, nq * share, rows), BF16),
                V((rows, width), BF16),
                V((2, nq, share, width), BF16),
                V((2, nq, share, width), BF16),
                V((nq, share, width), F32),
                V((nq, share, width), BF16),
                V((nq, share, width), BF16),
                V((nq, share, width), BF16),
                V((nq, share, width), BF16),
                V((nq, share, width), BF16),
                S((5,)), S((nq,)), S((nq,)), S((nq,)), S((nq,)), S((nq,)), S((nq, 2)), S((nq, 2)),
                S((nq,)), S((nq,)), S((3,)), S((3,)),
                S((2,)), S((2,)), S((nq,)), S((nq,)), S((nq,)), S((nq,)), S((nq,)), S((nq,)),
            ],
            compiler_params=pltpu.CompilerParams(
                collective_id=0, has_side_effects=True, vmem_limit_bytes=56 * 2**20
            ),
            name="contrast",
        )(
            write_pointer, slot_owner, positive_index.reshape(1, rows),
            query_inputs, key_inputs, query_weight, key_weight, queue_keys,
        )
        return loss.reshape(rows), grad, queue

    return body


def solution(mesh):
    in_specs = (
        P(("groups", "queue", "dp"), None),
        P(("groups", "queue", "dp"), None),
        P(),
        P(),
        P(("groups", "queue"), None),
        P("groups"),
        P("groups"),
        P(("groups", "queue", "dp")),
    )
    out_specs = (
        P(("groups", "queue", "dp")),
        P(("groups", "queue", "dp"), None),
        P(("groups", "queue"), None),
    )
    body = make_body(mesh.shape["queue"], mesh.shape["dp"])
    return jax.shard_map(body, mesh=mesh, in_specs=in_specs, out_specs=out_specs, check_vma=False)
```

time: 194 us -> 52.8 us (0.27)
  waiting for transfers between devices: 126 us -> 0 us
  Pallas kernels: 0 us -> 46.5 us
  blocking collectives: 23.4 us -> 0 us
  between operations: 14.8 us -> 1.29 us
  matrix products: 12.5 us -> 0 us
  other arithmetic: 7.08 us -> 0 us
  local copies, waits for them, and re-layouts: 9.73 us -> 4.76 us
    psum x1 -> x0, waiting for transfers between devices: 79.1 us -> none  [body(): summed = lax.psum(term, ('queue', 'dp'))]
    pallas_call x0 -> x1, Pallas kernels: none -> 46.5 us  [body(): pl.pallas_call(functools.partial(kernel, nq, nd), out_shape=(jax.ShapeDty...]
    all_gather x1 -> x0, waiting for transfers between devices: 46.4 us -> none  [body(): lax.all_gather(queue_keys, 'queue', axis=0, tiled=True)]
    all_gather x1 -> x0, blocking collectives: 23.4 us -> none  [body(): arrived = lax.all_gather(fresh, ('queue', 'dp'), axis=0, tiled=True)]
    dot_general x5 -> x0, matrix products: 12.5 us -> none  [the longest x1 3.1 us: fold(): jnp.dot(expo.astype(jnp.bfloat16), piece, preferred_element_type=jnp.floa...]
    gather x3 -> x0, local copies, waits for them, and re-layouts: 5.99 us -> none  [the longest x1 4.21 us: fold(): jnp.take(piece, jnp.clip(mapped, 0, count - 1), axis=0).astype(jnp.float32)]
    select_n x3 -> x0, other arithmetic: 5.19 us -> none  [the longest x1 2.52 us: body(): jnp.take(arrived, source, axis=0)]
    unnamed x11 -> x3, local copies, waits for them, and re-layouts: 2.51 us -> 4.76 us
  transfers between devices with their start and end apart: 2 -> 0, of which waited for: 2 -> 0; matrix products, arithmetic and copies ran while one was open for 6% -> 0% of each run, Pallas kernels for 0% -> 0%
where the time goes in v1:
time: 52.8 us; the launch traced here: 52.5 us
  Pallas kernels  46.5 us (88%)
  local copies, waits for them, and re-layouts  4.76 us (9%)
  between operations  1.29 us (2%)
    pallas_call x1, Pallas kernels, body(): pl.pallas_call(functools.partial(kernel, nq, nd), out_shape=(jax.ShapeDty...  46.5 us
    unnamed x3, local copies, waits for them, and re-layouts  4.76 us

profile of v1, /device:TPU:0, one launch (start us, length us, event | category | flops | bytes accessed | tf_op | source)
XLA Modules:
  0.0 52.5 jit_solution(5518753835852241267)
XLA Ops:
  1.3 46.5 %contrast.1 = (f32[1,256]{1,0:T(1,128)}, f32[64,1024]{1,0:T(8,128)}, bf16[256,1024]{1,0:T(8,128)(2,1)}) custom-call(s32[1]{0:T(128)S(6)} %copy.14.pointer_ref, s32[16]{0:T(128)} %owner_ref.1, s32[1,256]{1,0:T(1,128)} %bitcast.2, bf16[256,1024]{1,0:T(8,128)(2,1)} %x_hbm.1, bf16[16,1024]{1,0:T(8,128)(2,1)} %kin_hbm.1, bf16[1024,1024]{1,0:T(8,128)(2,1)} %wq_hbm.1, ...), custom_call_target="tpu_custom_call" | custom-call | tf_op jit(solution)/shard_map/contrast/pallas_call | solution.py:404
  47.8 1.2 %copy.15 = f32[256]{0:T(256)} copy(f32[256]{0:T(256)} %bitcast.3) | data formatting | bytes 2048
  49.0 1.7 %copy.16 = f32[64,1024]{1,0:T(8,128)} copy(f32[64,1024]{1,0:T(8,128)} %get-tuple-element.13) | data formatting | bytes 524288
  50.7 1.9 %copy.17 = bf16[256,1024]{1,0:T(8,128)(2,1)} copy(bf16[256,1024]{1,0:T(8,128)(2,1)} %get-tuple-element.14) | data formatting | bytes 1048576

commit v2 on v1

v2 whole, which is shorter than its diff:
```python
import functools

import jax
import jax.numpy as jnp
from jax import lax
from jax.experimental import pallas as pl
from jax.experimental.pallas import tpu as pltpu
from jax.sharding import PartitionSpec as P

temper = 0.05
splits = 2
cuts = 4
MESH = pl.DeviceIdType.MESH
F32 = jnp.float32
BF16 = jnp.bfloat16


def dot(a, b, da, db):
    return lax.dot_general(a, b, (((da,), (db,)), ((), ())), preferred_element_type=F32)


def kernel(
    nq, nd,
    pointer_hbm, owner_hbm, index_hbm, x_hbm, kin_hbm, wq_hbm, wk_hbm, keys_hbm,
    loss_hbm, grad_hbm, queue_hbm,
    pointer_ref, owner_ref, index_ref, loss_ref, queue_ref,
    x_ref, kin_ref, wq_ref, wk_ref, keys, fresh,
    unit_f, unit, inv_len, top, total, posit, pos_col, mixture, chosen,
    xt, grad_q, core_out, core_in, keep_out, keep_in, part, x_out, x_in, up_in, down_in, z_out,
    load_sem, store_sem, up_send, down_send, z_recv, x_send, x_recv, c_send, c_recv,
    fz_send, fz_recv, f_send, f_recv,
    gc_send, gc_recv, gk_send, gk_recv, gx_send, gx_recv, gu_send, gd_send, gu_recv, gd_recv,
):
    q = lax.axis_index("queue")
    d = lax.axis_index("dp")
    hi, lo = d // 2, d % 2
    side = (1 - hi) * 2 + lo
    mate = hi * 2 + (1 - lo)
    cross = (1 - hi) * 2 + (1 - lo)
    rows, width = x_ref.shape
    n_keys = keys.shape[1]
    quarter = n_keys // nd
    new = kin_ref.shape[0]
    blocks = part.shape[0]
    sub = blocks // nq
    share = grad_hbm.shape[0]
    thin = share // sub
    cut = quarter // sub
    micro = (nq - 1) * sub

    loads = [
        pltpu.make_async_copy(src, dst, load_sem.at[i])
        for i, (src, dst) in enumerate(
            (
                (x_hbm, x_ref),
                (wq_hbm, wq_ref),
                (keys_hbm, keys.at[q]),
                (kin_hbm, kin_ref),
                (wk_hbm, wk_ref),
                (index_hbm, index_ref),
                (owner_hbm, owner_ref),
                (pointer_hbm, pointer_ref),
            )
        )
    ]
    for load in loads:
        load.start()

    def piece(k, part_of):
        start = part_of * quarter + lax.rem(k, sub) * cut
        return keys.at[k // sub, pl.ds(pl.multiple_of(start, cut), cut)]

    def remote(src, dst, send, recv, where):
        return pltpu.make_async_remote_copy(
            src_ref=src, dst_ref=dst, send_sem=send, recv_sem=recv,
            device_id=where, device_id_type=MESH,
        )

    above = {"queue": jnp.minimum(q + 1, nq - 1)}
    below = {"queue": jnp.maximum(q - 1, 0)}

    def own_piece(h):
        return keys_hbm.at[pl.ds(pl.multiple_of(d * quarter + h * cut, cut), cut)]

    def key_up(k, src=None):
        src = piece(k, d) if src is None else src
        return remote(src, piece(k, d), up_send.at[k], z_recv.at[k], above)

    def key_down(k, src=None):
        src = piece(k, d) if src is None else src
        return remote(src, piece(k, d), down_send.at[k], z_recv.at[k], below)

    def key_side(k):
        return remote(piece(k, d), piece(k, d), x_send.at[k], x_recv.at[k], {"dp": side})

    def key_side_in(k):
        return remote(piece(k, side), piece(k, side), x_send.at[k], x_recv.at[k], {"dp": side})

    def key_mate(k, i, part_of):
        return remote(piece(k, part_of), piece(k, part_of), c_send.at[k, i], c_recv.at[k, i], {"dp": mate})

    barrier = pltpu.get_barrier_semaphore()
    pl.semaphore_signal(barrier, inc=1, device_id={"dp": side}, device_id_type=MESH)
    pl.semaphore_signal(barrier, inc=1, device_id={"dp": mate}, device_id_type=MESH)
    for r in range(nq):
        @pl.when(q != r)
        def _():
            pl.semaphore_signal(barrier, inc=1, device_id={"queue": r}, device_id_type=MESH)
    pl.semaphore_wait(barrier, nq + 1)

    for h in range(sub):
        @pl.when(q < nq - 1)
        def _():
            key_up(q * sub + h, own_piece(h)).start()

        @pl.when(q > 0)
        def _():
            key_down(q * sub + h, own_piece(h)).start()

    loads[0].wait()
    loads[1].wait()
    query = jnp.dot(x_ref[...], wq_ref[...], preferred_element_type=F32)
    scale = lax.rsqrt(jnp.sum(query * query, -1, keepdims=True) + 1e-06)
    inv_len[...] = scale
    query = query * scale
    unit_f[...] = query
    unit[...] = query.astype(BF16)
    top[...] = jnp.full(top.shape, -1e30, F32)
    total[...] = jnp.zeros(total.shape, F32)
    posit[...] = jnp.zeros(posit.shape, F32)
    mixture[...] = jnp.zeros(mixture.shape, F32)
    chosen[...] = jnp.zeros(chosen.shape, F32)
    eye = lax.broadcasted_iota(jnp.int32, (rows, rows), 0) == lax.broadcasted_iota(
        jnp.int32, (rows, rows), 1
    )
    loads[5].wait()
    pos_col[...] = jnp.sum(jnp.where(eye, index_ref[...], 0), -1, keepdims=True)

    def fold(r):
        block = keys[r]
        scores = dot(unit[...], block, 1, 1) / temper
        hit = lax.broadcasted_iota(jnp.int32, (rows, n_keys), 1) + r * n_keys == pos_col[...]
        posit[...] += jnp.sum(jnp.where(hit, scores, 0.0), -1, keepdims=True)
        old = top[...]
        high = jnp.maximum(old, jnp.max(scores, -1, keepdims=True))
        decay = jnp.exp(old - high)
        expo = jnp.exp(scores - high)
        top[...] = high
        total[...] = total[...] * decay + jnp.sum(expo, -1, keepdims=True)
        mixture[...] = mixture[...] * decay + jnp.dot(
            expo.astype(BF16), block, preferred_element_type=F32
        )
        chosen[...] += jnp.dot(
            jnp.where(hit, 1.0, 0.0).astype(BF16), block, preferred_element_type=F32
        )

    def make_fresh():
        loads[3].wait()
        loads[4].wait()
        made = jnp.dot(kin_ref[...], wk_ref[...], preferred_element_type=F32)
        made = (made * lax.rsqrt(jnp.sum(made * made, -1, keepdims=True) + 1e-06)).astype(BF16)
        fresh[d, pl.ds(pl.multiple_of(q * new, new), new)] = made

    def fresh_out(r):
        slot = fresh.at[d, pl.ds(pl.multiple_of(q * new, new), new)]
        return remote(slot, slot, fz_send.at[r], fz_recv.at[q], {"queue": r})

    def fresh_in(r):
        slot = fresh.at[d, pl.ds(pl.multiple_of(r * new, new), new)]
        return remote(slot, slot, fz_send.at[r], fz_recv.at[r], {"queue": r})

    def fresh_move(k, part_of, where):
        return remote(fresh.at[part_of], fresh.at[part_of], f_send.at[k], f_recv.at[k], {"dp": where})

    def turn():
        turned = x_ref[...].astype(F32).T
        for p in range(nd):
            xt[p] = jnp.concatenate(
                [turned[(r * nd + p) * share : (r * nd + p + 1) * share] for r in range(nq)], axis=0
            ).astype(BF16)

    loads[2].wait()
    fold(q)

    def others(m, act):
        s, h = m // sub + 1, lax.rem(m, sub)

        @pl.when(q - s >= 0)
        def _():
            act((q - s) * sub + h, True)

        @pl.when(q + s <= nq - 1)
        def _():
            act((q + s) * sub + h, False)

    def pass_on(k, upward):
        key_up(k).wait_recv()
        if upward:
            @pl.when(q < nq - 1)
            def _():
                key_up(k).start()
        else:
            @pl.when(q > 0)
            def _():
                key_down(k).start()
        key_side(k).start()
        key_mate(k, 0, d).start()

    def pass_side(k, upward):
        key_side_in(k).wait_recv()
        key_mate(k, 1, side).start()

    def step(m, carry):
        @pl.when(m < micro)
        def _():
            others(m, pass_on)

        @pl.when(m == 0)
        def _():
            make_fresh()

        @pl.when(m == 1)
        def _():
            turn()

        @pl.when(m == micro - 1)
        def _():
            for r in range(nq):
                @pl.when(q != r)
                def _():
                    fresh_out(r).start()

        @pl.when((m >= 2) & (m < micro + 2))
        def _():
            others(m - 2, pass_side)

        @pl.when((m >= 3) & (lax.rem(m, sub) == (sub + 2) % sub))
        def _():
            def both(i, carry):
                r = q + ((m - 3) // sub + 1) * (2 * i - 1)

                @pl.when((r >= 0) & (r <= nq - 1))
                def _():
                    for h in range(sub):
                        key_mate(r * sub + h, 0, mate).wait_recv()
                        key_mate(r * sub + h, 1, cross).wait_recv()
                    fold(r)

                return carry

            lax.fori_loop(0, 2, both, 0)

        return carry

    lax.fori_loop(0, micro + 3, step, 0)

    for r in range(nq):
        @pl.when(q != r)
        def _():
            fresh_in(r).wait_recv()
    fresh_move(0, d, side).start()
    fresh_move(1, d, mate).start()

    count = total[...]
    grad_unit = mixture[...] * (1.0 / (count * temper)) - chosen[...] * (1.0 / temper)
    units = unit_f[...]
    grad_q[...] = (
        (grad_unit - units * jnp.sum(units * grad_unit, -1, keepdims=True)) * inv_len[...]
    ).astype(BF16)

    def term(p):
        return jnp.dot(xt[p], grad_q[...], preferred_element_type=F32).reshape(blocks, thin, width)

    def grad_mate(k):
        return remote(core_out.at[k], core_in.at[k], gc_send.at[k], gc_recv.at[k], {"dp": mate})

    def grad_keep():
        return remote(keep_out, keep_in, gk_send.at[0], gk_recv.at[0], {"dp": mate})

    def grad_side(k):
        return remote(x_out.at[k], x_in.at[k], gx_send.at[k], gx_recv.at[k], {"dp": side})

    def grad_up(k):
        return remote(z_out.at[k], up_in.at[k], gu_send.at[k], gu_recv.at[k], above)

    def grad_down(k):
        return remote(z_out.at[k], down_in.at[k], gd_send.at[k], gd_recv.at[k], below)

    def in_turn(act_up, act_down, act_own):
        def at(t, carry):
            for_up = nq - 1 - (t - q)
            for_down = t - (nq - 1 - q)
            for h in range(sub):
                @pl.when((t >= q) & (for_up > q))
                def _():
                    act_up(for_up * sub + h)

                @pl.when((for_down >= 0) & (for_down < q))
                def _():
                    act_down(for_down * sub + h)

            return carry

        lax.fori_loop(0, nq - 1, at, 0)
        for h in range(sub):
            act_own(q * sub + h)

    def start_mate(k):
        grad_mate(k).start()

    core_out[...] = term(cross).astype(BF16)
    in_turn(start_mate, start_mate, start_mate)
    part[...] = term(side)
    keep_out[...] = term(mate).astype(BF16)
    grad_keep().start()

    def start_side(k):
        grad_mate(k).wait_recv()
        x_out[k] = (part[k] + core_in[k].astype(F32)).astype(BF16)
        grad_side(k).start()

    in_turn(start_side, start_side, start_side)
    fresh_move(0, side, side).wait_recv()
    fresh_move(2, side, mate).start()
    part[...] = term(d)
    grad_keep().wait_recv()
    part[...] += keep_in[...].astype(F32)

    loss_col = top[...] + jnp.log(count) - posit[...]
    loss_ref[...] = jnp.sum(jnp.where(eye, loss_col, 0.0), 0, keepdims=True)
    stores = [
        pltpu.make_async_copy(loss_ref, loss_hbm, store_sem.at[0]),
        pltpu.make_async_copy(queue_ref, queue_hbm, store_sem.at[1]),
    ]
    stores[0].start()

    loads[6].wait()
    loads[7].wait()
    fresh_move(1, mate, mate).wait_recv()
    fresh_move(2, cross, mate).wait_recv()
    n_new = nd * nq * new
    column = lax.broadcasted_iota(jnp.int32, (1, n_new), 1)
    block = (column % (nq * new)) // new * nd + column // (nq * new)
    goes = jnp.zeros((1, n_new), jnp.int32)
    for b in range(nd * nq):
        goes = jnp.where(block == b, owner_ref[b], goes)
    goes = goes * new + column % new - q * (nd * new)
    offset = lax.broadcasted_iota(jnp.int32, (n_keys, 1), 0) - pointer_ref[0]
    offset = jnp.where(offset < 0, offset + n_keys, offset)
    pick = jnp.where((goes == offset) & (offset < nd * new), 1.0, 0.0).astype(BF16)
    moved = jnp.dot(pick, fresh[...].reshape(n_new, width), preferred_element_type=F32)
    queue_ref[...] = jnp.where(offset < nd * new, moved, keys[q].astype(F32)).astype(BF16)

    stores[1].start()

    def up_step(k):
        grad_side(k).wait_recv()
        part[k] += x_in[k].astype(F32)

        @pl.when(q > 0)
        def _():
            grad_up(k).wait_recv()
            part[k] += up_in[k].astype(F32)

        z_out[k] = part[k].astype(BF16)
        grad_up(k).start()

    def down_step(k):
        grad_side(k).wait_recv()
        part[k] += x_in[k].astype(F32)

        @pl.when(q < nq - 1)
        def _():
            grad_down(k).wait_recv()
            part[k] += down_in[k].astype(F32)

        z_out[k] = part[k].astype(BF16)
        grad_down(k).start()

    def own_out(h):
        return pltpu.make_async_copy(
            part.at[q * sub + h], grad_hbm.at[pl.ds(h * thin, thin)], store_sem.at[2 + h]
        )

    def own_step(k):
        grad_side(k).wait_recv()
        part[k] += x_in[k].astype(F32)

        @pl.when(q > 0)
        def _():
            grad_up(k).wait_recv()
            part[k] += up_in[k].astype(F32)

        @pl.when(q < nq - 1)
        def _():
            grad_down(k).wait_recv()
            part[k] += down_in[k].astype(F32)

    in_turn(up_step, down_step, lambda k: None)
    for h in range(sub):
        own_step(q * sub + h)
        own_out(h).start()

    def drain(k, carry):
        r = k // sub

        @pl.when((r <= q) & (q < nq - 1))
        def _():
            key_up(k).wait_send()

        @pl.when((r >= q) & (q > 0))
        def _():
            key_down(k).wait_send()

        @pl.when(r != q)
        def _():
            key_side(k).wait_send()
            key_mate(k, 0, d).wait_send()
            key_mate(k, 1, side).wait_send()

        grad_mate(k).wait_send()
        grad_side(k).wait_send()

        @pl.when(r > q)
        def _():
            grad_up(k).wait_send()

        @pl.when(r < q)
        def _():
            grad_down(k).wait_send()

        return carry

    lax.fori_loop(0, blocks, drain, 0)
    for r in range(nq):
        @pl.when(q != r)
        def _():
            fresh_out(r).wait_send()
    fresh_move(0, d, side).wait_send()
    fresh_move(1, d, mate).wait_send()
    fresh_move(2, side, mate).wait_send()
    grad_keep().wait_send()
    for store in stores:
        store.wait()
    for h in range(sub):
        own_out(h).wait()


def finish(cuts, loss_in, grad_in, queue_in, loss_out, grad_out, queue_out, sem):
    copies = [pltpu.make_async_copy(loss_in, loss_out, sem.at[0])]
    for src, dst in ((grad_in, grad_out), (queue_in, queue_out)):
        n = src.shape[0] // cuts if src.shape[0] % (16 * cuts) == 0 else src.shape[0]
        for at in range(0, src.shape[0], n):
            piece = pl.ds(at, n)
            copies.append(pltpu.make_async_copy(src.at[piece], dst.at[piece], sem.at[len(copies)]))
    for copy in copies:
        copy.start()
    for copy in copies:
        copy.wait()


def make_body(nq, nd):

    def body(
        query_inputs, key_inputs, query_weight, key_weight,
        queue_keys, write_pointer, slot_owner, positive_index,
    ):
        rows, width = query_inputs.shape
        n_keys = queue_keys.shape[0]
        new = key_inputs.shape[0]
        share = width // (nq * nd)
        sub = splits if share % (16 * splits) == 0 else 1
        blocks, thin = nq * sub, share // sub
        hbm = pl.BlockSpec(memory_space=pl.ANY)
        V = pltpu.VMEM
        S = pltpu.SemaphoreType.DMA
        outs = (
            jax.ShapeDtypeStruct((1, rows), F32),
            jax.ShapeDtypeStruct((share, width), F32),
            jax.ShapeDtypeStruct((n_keys, width), BF16),
        )
        each = S((blocks,))
        made = pl.pallas_call(
            functools.partial(kernel, nq, nd),
            out_shape=outs,
            in_specs=[hbm] * 8,
            out_specs=(hbm,) * 3,
            scratch_shapes=[
                pltpu.SMEM(write_pointer.shape, jnp.int32),
                pltpu.SMEM(slot_owner.shape, jnp.int32),
                V((1, rows), jnp.int32),
                V((1, rows), F32),
                V((n_keys, width), BF16),
                V((rows, width), BF16),
                V((new, width), BF16),
                V(query_weight.shape, BF16),
                V(key_weight.shape, BF16),
                V((nq, n_keys, width), BF16),
                V((nd, nq * new, width), BF16),
                V((rows, width), F32),
                V((rows, width), BF16),
                V((rows, 1), F32),
                V((rows, 1), F32),
                V((rows, 1), F32),
                V((rows, 1), F32),
                V((rows, 1), jnp.int32),
                V((rows, width), F32),
                V((rows, width), F32),
                V((nd, nq * share, rows), BF16),
                V((rows, width), BF16),
                V((blocks, thin, width), BF16),
                V((blocks, thin, width), BF16),
                V((blocks, thin, width), BF16),
                V((blocks, thin, width), BF16),
                V((blocks, thin, width), F32),
                V((blocks, thin, width), BF16),
                V((blocks, thin, width), BF16),
                V((blocks, thin, width), BF16),
                V((blocks, thin, width), BF16),
                V((blocks, thin, width), BF16),
                S((8,)), S((2 + sub,)), each, each, each, each, each, S((blocks, 2)), S((blocks, 2)),
                S((nq,)), S((nq,)), S((3,)), S((3,)),
                each, each, S((1,)), S((1,)), each, each, each, each, each, each,
            ],
            compiler_params=pltpu.CompilerParams(
                collective_id=0, has_side_effects=True, vmem_limit_bytes=56 * 2**20
            ),
            name="contrast",
        )(
            write_pointer, slot_owner, positive_index.reshape(1, rows),
            query_inputs, key_inputs, query_weight, key_weight, queue_keys,
        )
        loss, grad, queue = pl.pallas_call(
            functools.partial(finish, cuts),
            out_shape=outs,
            in_specs=[hbm] * 3,
            out_specs=(hbm,) * 3,
            scratch_shapes=[S((1 + 2 * cuts,))],
            name="finish",
        )(*made)
        return loss.reshape(rows), grad, queue

    return body


def solution(mesh):
    in_specs = (
        P(("groups", "queue", "dp"), None),
        P(("groups", "queue", "dp"), None),
        P(),
        P(),
        P(("groups", "queue"), None),
        P("groups"),
        P("groups"),
        P(("groups", "queue", "dp")),
    )
    out_specs = (
        P(("groups", "queue", "dp")),
        P(("groups", "queue", "dp"), None),
        P(("groups", "queue"), None),
    )
    body = make_body(mesh.shape["queue"], mesh.shape["dp"])
    return jax.shard_map(body, mesh=mesh, in_specs=in_specs, out_specs=out_specs, check_vma=False)
```

time: 52.8 us -> 71.1 us (1.35)
  Pallas kernels: 46.5 us -> 69.7 us
  local copies, waits for them, and re-layouts: 4.76 us -> 0 us
    pallas_call x1 -> x2, Pallas kernels: 46.5 us -> 69.7 us  [the longest x1 44.6 us: body(): pl.pallas_call(functools.partial(kernel, nq, nd), out_shape=outs, in_spec...]
    unnamed x3 -> x0, local copies, waits for them, and re-layouts: 4.76 us -> none
where the time goes in v2:
time: 71.1 us; the launch traced here: 71 us
  Pallas kernels  69.7 us (98%)
  between operations  1.29 us (2%)
    pallas_call x1, Pallas kernels, body(): pl.pallas_call(functools.partial(kernel, nq, nd), out_shape=outs, in_spec...  44.6 us
    pallas_call x1, Pallas kernels, body(): pl.pallas_call(functools.partial(finish, cuts), out_shape=outs, in_specs=...  25 us

profile of v2, /device:TPU:0, one launch (start us, length us, event | category | flops | bytes accessed | tf_op | source)
XLA Modules:
  0.0 71.0 jit_solution(6703900122738633656)
XLA Ops:
  1.3 44.6 %contrast.1 = (f32[1,256]{1,0:T(1,128)}, f32[64,1024]{1,0:T(8,128)}, bf16[256,1024]{1,0:T(8,128)(2,1)}) custom-call(s32[1]{0:T(128)S(6)} %copy.11.pointer_hbm, s32[16]{0:T(128)} %owner_hbm.1, s32[1,256]{1,0:T(1,128)} %bitcast.2, bf16[256,1024]{1,0:T(8,128)(2,1)} %x_hbm.1, bf16[16,1024]{1,0:T(8,128)(2,1)} %kin_hbm.1, bf16[1024,1024]{1,0:T(8,128)(2,1)} %wq_hbm.1, ...), custom_call_target="tpu_custom_call" | custom-call | tf_op jit(solution)/shard_map/contrast/pallas_call | solution.py:483
  45.9 25.0 %finish.1 = (f32[1,256]{1,0:T(1,128)}, f32[64,1024]{1,0:T(8,128)}, bf16[256,1024]{1,0:T(8,128)(2,1)}) custom-call(f32[1,256]{1,0:T(1,128)} %get-tuple-element.9.loss_in, f32[64,1024]{1,0:T(8,128)} %get-tuple-element.10.grad_in, bf16[256,1024]{1,0:T(8,128)(2,1)} %get-tuple-element.11.queue_in), custom_call_target="tpu_custom_call" | custom-call | tf_op jit(solution)/shard_map/finish/pallas_call | solution.py:533

commit v3 on v2

--- a/solution.py
+++ b/solution.py
@@ -9,7 +9,8 @@
 
 temper = 0.05
 splits = 2
-cuts = 4
+tile = 256
+strip = 32
 MESH = pl.DeviceIdType.MESH
 F32 = jnp.float32
 BF16 = jnp.bfloat16
@@ -23,7 +24,7 @@
     nq, nd,
     pointer_hbm, owner_hbm, index_hbm, x_hbm, kin_hbm, wq_hbm, wk_hbm, keys_hbm,
     loss_hbm, grad_hbm, queue_hbm,
-    pointer_ref, owner_ref, index_ref, loss_ref, queue_ref,
+    pointer_ref, owner_ref, index_ref, loss_ref, queue_ref, pair, fade, made_f, picks,
     x_ref, kin_ref, wq_ref, wk_ref, keys, fresh,
     unit_f, unit, inv_len, top, total, posit, pos_col, mixture, chosen,
     xt, grad_q, core_out, core_in, keep_out, keep_in, part, x_out, x_in, up_in, down_in, z_out,
@@ -119,17 +120,29 @@
 
     loads[0].wait()
     loads[1].wait()
-    query = jnp.dot(x_ref[...], wq_ref[...], preferred_element_type=F32)
-    scale = lax.rsqrt(jnp.sum(query * query, -1, keepdims=True) + 1e-06)
-    inv_len[...] = scale
-    query = query * scale
-    unit_f[...] = query
-    unit[...] = query.astype(BF16)
+    inv_len[...] = jnp.zeros(inv_len.shape, F32)
+
+    @pl.loop(0, width // tile)
+    def _(j):
+        cols = pl.ds(pl.multiple_of(j * tile, tile), tile)
+        query = jnp.dot(x_ref[...], wq_ref[:, cols], preferred_element_type=F32)
+        unit_f[:, cols] = query
+        inv_len[...] += jnp.sum(query * query, -1, keepdims=True)
+
+    inv_len[...] = lax.rsqrt(inv_len[...] + 1e-06)
+
+    @pl.loop(0, rows // strip)
+    def _(i):
+        at = pl.ds(pl.multiple_of(i * strip, strip), strip)
+        query = unit_f[at] * inv_len[at]
+        unit_f[at] = query
+        unit[at] = query.astype(BF16)
+        mixture[at] = jnp.zeros((strip, width), F32)
+        chosen[at] = jnp.zeros((strip, width), F32)
+
     top[...] = jnp.full(top.shape, -1e30, F32)
     total[...] = jnp.zeros(total.shape, F32)
     posit[...] = jnp.zeros(posit.shape, F32)
-    mixture[...] = jnp.zeros(mixture.shape, F32)
-    chosen[...] = jnp.zeros(chosen.shape, F32)
     eye = lax.broadcasted_iota(jnp.int32, (rows, rows), 0) == lax.broadcasted_iota(
         jnp.int32, (rows, rows), 1
     )
@@ -147,17 +160,28 @@
         expo = jnp.exp(scores - high)
         top[...] = high
         total[...] = total[...] * decay + jnp.sum(expo, -1, keepdims=True)
-        mixture[...] = mixture[...] * decay + jnp.dot(
-            expo.astype(BF16), block, preferred_element_type=F32
-        )
-        chosen[...] += jnp.dot(
-            jnp.where(hit, 1.0, 0.0).astype(BF16), block, preferred_element_type=F32
-        )
+        pair[:rows] = expo.astype(BF16)
+        pair[rows:] = jnp.where(hit, 1.0, 0.0).astype(BF16)
+        fade[...] = decay
+
+        @pl.loop(0, width // tile)
+        def _(j):
+            cols = pl.ds(pl.multiple_of(j * tile, tile), tile)
+            both = jnp.dot(pair[...], keys[r, :, cols], preferred_element_type=F32)
+            mixture[:, cols] = mixture[:, cols] * fade[...] + both[:rows]
+            chosen[:, cols] += both[rows:]
+
 
     def make_fresh():
         loads[3].wait()
         loads[4].wait()
-        made = jnp.dot(kin_ref[...], wk_ref[...], preferred_element_type=F32)
+
+        @pl.loop(0, width // tile)
+        def _(j):
+            cols = pl.ds(pl.multiple_of(j * tile, tile), tile)
+            made_f[:, cols] = jnp.dot(kin_ref[...], wk_ref[:, cols], preferred_element_type=F32)
+
+        made = made_f[...]
         made = (made * lax.rsqrt(jnp.sum(made * made, -1, keepdims=True) + 1e-06)).astype(BF16)
         fresh[d, pl.ds(pl.multiple_of(q * new, new), new)] = made
 
@@ -173,14 +197,20 @@
         return remote(fresh.at[part_of], fresh.at[part_of], f_send.at[k], f_recv.at[k], {"dp": where})
 
     def turn():
+        if nd * share % 128 == 0:
+            @pl.loop(0, nq)
+            def _(r):
+                cols = pl.ds(pl.multiple_of(r * nd * share, nd * share), nd * share)
+                turned = x_ref[:, cols].astype(F32).T.astype(BF16)
+                for p in range(nd):
+                    xt[p, pl.ds(pl.multiple_of(r * share, share), share)] = turned[p * share : (p + 1) * share]
+
+            return
         turned = x_ref[...].astype(F32).T
         for p in range(nd):
             xt[p] = jnp.concatenate(
                 [turned[(r * nd + p) * share : (r * nd + p + 1) * share] for r in range(nq)], axis=0
             ).astype(BF16)
-
-    loads[2].wait()
-    fold(q)
 
     def others(m, act):
         s, h = m // sub + 1, lax.rem(m, sub)
@@ -234,21 +264,28 @@
         def _():
             others(m - 2, pass_side)
 
-        @pl.when((m >= 3) & (lax.rem(m, sub) == (sub + 2) % sub))
-        def _():
-            def both(i, carry):
-                r = q + ((m - 3) // sub + 1) * (2 * i - 1)
-
-                @pl.when((r >= 0) & (r <= nq - 1))
-                def _():
-                    for h in range(sub):
-                        key_mate(r * sub + h, 0, mate).wait_recv()
-                        key_mate(r * sub + h, 1, cross).wait_recv()
-                    fold(r)
-
-                return carry
-
-            lax.fori_loop(0, 2, both, 0)
+        @pl.when(m == 0)
+        def _():
+            loads[2].wait()
+
+        def both(i, carry):
+            r = jnp.where(m == 0, q, q + ((m - 3) // sub + 1) * (2 * i - 1))
+            own = (m == 0) & (i == 0)
+            later = (m >= 3) & (lax.rem(m, sub) == 2 % sub) & (r >= 0) & (r <= nq - 1)
+
+            @pl.when(later)
+            def _():
+                for h in range(sub):
+                    key_mate(r * sub + h, 0, mate).wait_recv()
+                    key_mate(r * sub + h, 1, cross).wait_recv()
+
+            @pl.when(own | later)
+            def _():
+                fold(r)
+
+            return carry
+
+        lax.fori_loop(0, 2, both, 0)
 
         return carry
 
@@ -261,15 +298,21 @@
     fresh_move(0, d, side).start()
     fresh_move(1, d, mate).start()
 
-    count = total[...]
-    grad_unit = mixture[...] * (1.0 / (count * temper)) - chosen[...] * (1.0 / temper)
-    units = unit_f[...]
-    grad_q[...] = (
-        (grad_unit - units * jnp.sum(units * grad_unit, -1, keepdims=True)) * inv_len[...]
-    ).astype(BF16)
-
-    def term(p):
-        return jnp.dot(xt[p], grad_q[...], preferred_element_type=F32).reshape(blocks, thin, width)
+    @pl.loop(0, rows // strip)
+    def _(i):
+        at = pl.ds(pl.multiple_of(i * strip, strip), strip)
+        grad_unit = mixture[at] * (1.0 / (total[at] * temper)) - chosen[at] * (1.0 / temper)
+        units = unit_f[at]
+        grad_q[at] = (
+            (grad_unit - units * jnp.sum(units * grad_unit, -1, keepdims=True)) * inv_len[at]
+        ).astype(BF16)
+
+    def term(p, out):
+        @pl.loop(0, width // tile)
+        def _(j):
+            cols = pl.ds(pl.multiple_of(j * tile, tile), tile)
+            got = jnp.dot(xt[p], grad_q[:, cols], preferred_element_type=F32)
+            out[:, :, cols] = got.reshape(blocks, thin, tile).astype(out.dtype)
 
     def grad_mate(k):
         return remote(core_out.at[k], core_in.at[k], gc_send.at[k], gc_recv.at[k], {"dp": mate})
@@ -290,7 +333,8 @@
         def at(t, carry):
             for_up = nq - 1 - (t - q)
             for_down = t - (nq - 1 - q)
-            for h in range(sub):
+
+            def half(h, carry):
                 @pl.when((t >= q) & (for_up > q))
                 def _():
                     act_up(for_up * sub + h)
@@ -299,6 +343,9 @@
                 def _():
                     act_down(for_down * sub + h)
 
+                return carry
+
+            lax.fori_loop(0, sub, half, 0)
             return carry
 
         lax.fori_loop(0, nq - 1, at, 0)
@@ -308,10 +355,10 @@
     def start_mate(k):
         grad_mate(k).start()
 
-    core_out[...] = term(cross).astype(BF16)
+    term(cross, core_out)
     in_turn(start_mate, start_mate, start_mate)
-    part[...] = term(side)
-    keep_out[...] = term(mate).astype(BF16)
+    term(side, part)
+    term(mate, keep_out)
     grad_keep().start()
 
     def start_side(k):
@@ -322,11 +369,14 @@
     in_turn(start_side, start_side, start_side)
     fresh_move(0, side, side).wait_recv()
     fresh_move(2, side, mate).start()
-    part[...] = term(d)
+    term(d, part)
     grad_keep().wait_recv()
-    part[...] += keep_in[...].astype(F32)
-
-    loss_col = top[...] + jnp.log(count) - posit[...]
+
+    @pl.loop(0, blocks)
+    def _(k):
+        part[k] += keep_in[k].astype(F32)
+
+    loss_col = top[...] + jnp.log(total[...]) - posit[...]
     loss_ref[...] = jnp.sum(jnp.where(eye, loss_col, 0.0), 0, keepdims=True)
     stores = [
         pltpu.make_async_copy(loss_ref, loss_hbm, store_sem.at[0]),
@@ -348,8 +398,18 @@
     offset = lax.broadcasted_iota(jnp.int32, (n_keys, 1), 0) - pointer_ref[0]
     offset = jnp.where(offset < 0, offset + n_keys, offset)
     pick = jnp.where((goes == offset) & (offset < nd * new), 1.0, 0.0).astype(BF16)
-    moved = jnp.dot(pick, fresh[...].reshape(n_new, width), preferred_element_type=F32)
-    queue_ref[...] = jnp.where(offset < nd * new, moved, keys[q].astype(F32)).astype(BF16)
+    picks[...] = pick
+
+    @pl.loop(0, width // tile)
+    def _(j):
+        cols = pl.ds(pl.multiple_of(j * tile, tile), tile)
+        moved = jnp.dot(
+            picks[...], fresh[:, :, cols].reshape(n_new, tile), preferred_element_type=F32
+        )
+        queue_ref[:, cols] = jnp.where(
+            offset < nd * new, moved, keys[q, :, cols].astype(F32)
+        ).astype(BF16)
+
 
     stores[1].start()
 
@@ -446,17 +506,10 @@
         own_out(h).wait()
 
 
-def finish(cuts, loss_in, grad_in, queue_in, loss_out, grad_out, queue_out, sem):
-    copies = [pltpu.make_async_copy(loss_in, loss_out, sem.at[0])]
-    for src, dst in ((grad_in, grad_out), (queue_in, queue_out)):
-        n = src.shape[0] // cuts if src.shape[0] % (16 * cuts) == 0 else src.shape[0]
-        for at in range(0, src.shape[0], n):
-            piece = pl.ds(at, n)
-            copies.append(pltpu.make_async_copy(src.at[piece], dst.at[piece], sem.at[len(copies)]))
-    for copy in copies:
-        copy.start()
-    for copy in copies:
-        copy.wait()
+def finish(loss_in, grad_in, queue_in, loss_out, grad_out, queue_out):
+    loss_out[...] = loss_in[...]
+    grad_out[...] = grad_in[...]
+    queue_out[...] = queue_in[...]
 
 
 def make_body(nq, nd):
@@ -471,6 +524,7 @@
         share = width // (nq * nd)
         sub = splits if share % (16 * splits) == 0 else 1
         blocks, thin = nq * sub, share // sub
+        vmem = pl.BlockSpec(memory_space=pltpu.VMEM)
         hbm = pl.BlockSpec(memory_space=pl.ANY)
         V = pltpu.VMEM
         S = pltpu.SemaphoreType.DMA
@@ -491,6 +545,10 @@
                 V((1, rows), jnp.int32),
                 V((1, rows), F32),
                 V((n_keys, width), BF16),
+                V((2 * rows, n_keys), BF16),
+                V((rows, 1), F32),
+                V((new, width), F32),
+                V((n_keys, nd * nq * new), BF16),
                 V((rows, width), BF16),
                 V((new, width), BF16),
                 V(query_weight.shape, BF16),
@@ -531,11 +589,10 @@
             query_inputs, key_inputs, query_weight, key_weight, queue_keys,
         )
         loss, grad, queue = pl.pallas_call(
-            functools.partial(finish, cuts),
+            finish,
             out_shape=outs,
-            in_specs=[hbm] * 3,
-            out_specs=(hbm,) * 3,
-            scratch_shapes=[S((1 + 2 * cuts,))],
+            in_specs=[vmem] * 3,
+            out_specs=(vmem,) * 3,
             name="finish",
         )(*made)
         return loss.reshape(rows), grad, queue

time: 71.1 us -> 50.5 us (0.71)
  Pallas kernels: 69.7 us -> 49.1 us
    pallas_call x1, Pallas kernels: 25 us -> 2.03 us  [body(): pl.pallas_call(finish, out_shape=outs, in_specs=[vmem] * 3, out_specs=(vm...]
    pallas_call x1, Pallas kernels: 44.6 us -> 47 us  [body(): pl.pallas_call(functools.partial(kernel, nq, nd), out_shape=outs, in_spec...]
where the time goes in v3:
time: 50.5 us; the launch traced here: 50.3 us
  Pallas kernels  49.1 us (97%)
  between operations  1.29 us (3%)
    pallas_call x1, Pallas kernels, body(): pl.pallas_call(functools.partial(kernel, nq, nd), out_shape=outs, in_spec...  47 us
    pallas_call x1, Pallas kernels, body(): pl.pallas_call(finish, out_shape=outs, in_specs=[vmem] * 3, out_specs=(vm...  2.03 us

profile of v3, /device:TPU:0, one launch (start us, length us, event | category | flops | bytes accessed | tf_op | source)
XLA Modules:
  0.0 50.3 jit_solution(1278298426259814278)
XLA Ops:
  1.3 47.0 %contrast.1 = (f32[1,256]{1,0:T(1,128)}, f32[64,1024]{1,0:T(8,128)}, bf16[256,1024]{1,0:T(8,128)(2,1)}) custom-call(s32[1]{0:T(128)S(6)} %copy.11.pointer_hbm, s32[16]{0:T(128)} %owner_hbm.1, s32[1,256]{1,0:T(1,128)} %bitcast.2, bf16[256,1024]{1,0:T(8,128)(2,1)} %x_hbm.1, bf16[16,1024]{1,0:T(8,128)(2,1)} %kin_hbm.1, bf16[1024,1024]{1,0:T(8,128)(2,1)} %wq_hbm.1, ...), custom_call_target="tpu_custom_call" | custom-call | tf_op jit(solution)/shard_map/contrast/pallas_call | solution.py:537
  48.3 2.0 %finish.1 = (f32[1,256]{1,0:T(1,128)}, f32[64,1024]{1,0:T(8,128)}, bf16[256,1024]{1,0:T(8,128)(2,1)}) custom-call(f32[1,256]{1,0:T(1,128)} %get-tuple-element.9.loss_in, f32[64,1024]{1,0:T(8,128)} %get-tuple-element.10.grad_in, bf16[256,1024]{1,0:T(8,128)(2,1)} %get-tuple-element.11.queue_in), custom_call_target="tpu_custom_call" | custom-call | tf_op jit(solution)/shard_map/finish/pallas_call | solution.py:591

commit v4 on v3

--- a/solution.py
+++ b/solution.py
@@ -9,7 +9,7 @@
 
 temper = 0.05
 splits = 2
-tile = 256
+tile = 512
 strip = 32
 MESH = pl.DeviceIdType.MESH
 F32 = jnp.float32
@@ -27,10 +27,10 @@
     pointer_ref, owner_ref, index_ref, loss_ref, queue_ref, pair, fade, made_f, picks,
     x_ref, kin_ref, wq_ref, wk_ref, keys, fresh,
     unit_f, unit, inv_len, top, total, posit, pos_col, mixture, chosen,
-    xt, grad_q, core_out, core_in, keep_out, keep_in, part, x_out, x_in, up_in, down_in, z_out,
-    load_sem, store_sem, up_send, down_send, z_recv, x_send, x_recv, c_send, c_recv,
+    xt, grad_q, core_out, core_in, keep_out, keep_in, part, x_out, x_in, z_in, z_out,
+    load_sem, store_sem, up_send, z_recv, x_send, x_recv, c_send, c_recv,
     fz_send, fz_recv, f_send, f_recv,
-    gc_send, gc_recv, gk_send, gk_recv, gx_send, gx_recv, gu_send, gd_send, gu_recv, gd_recv,
+    gc_send, gc_recv, gk_send, gk_recv, gx_send, gx_recv, gu_send, gu_recv,
 ):
     q = lax.axis_index("queue")
     d = lax.axis_index("dp")
@@ -77,19 +77,17 @@
             device_id=where, device_id_type=MESH,
         )
 
-    above = {"queue": jnp.minimum(q + 1, nq - 1)}
-    below = {"queue": jnp.maximum(q - 1, 0)}
-
     def own_piece(h):
         return keys_hbm.at[pl.ds(pl.multiple_of(d * quarter + h * cut, cut), cut)]
 
-    def key_up(k, src=None):
-        src = piece(k, d) if src is None else src
-        return remote(src, piece(k, d), up_send.at[k], z_recv.at[k], above)
-
-    def key_down(k, src=None):
-        src = piece(k, d) if src is None else src
-        return remote(src, piece(k, d), down_send.at[k], z_recv.at[k], below)
+    def key_out(r, h):
+        return remote(
+            own_piece(h), piece(q * sub + h, d), up_send.at[r * sub + h], z_recv.at[q * sub + h],
+            {"queue": r},
+        )
+
+    def key_in(k):
+        return remote(piece(k, d), piece(k, d), up_send.at[k], z_recv.at[k], {"queue": k // sub})
 
     def key_side(k):
         return remote(piece(k, d), piece(k, d), x_send.at[k], x_recv.at[k], {"dp": side})
@@ -109,14 +107,20 @@
             pl.semaphore_signal(barrier, inc=1, device_id={"queue": r}, device_id_type=MESH)
     pl.semaphore_wait(barrier, nq + 1)
 
-    for h in range(sub):
-        @pl.when(q < nq - 1)
-        def _():
-            key_up(q * sub + h, own_piece(h)).start()
-
-        @pl.when(q > 0)
-        def _():
-            key_down(q * sub + h, own_piece(h)).start()
+    def others(m, act):
+        s, h = m // sub + 1, lax.rem(m, sub)
+
+        @pl.when(q - s >= 0)
+        def _():
+            act(q - s, h)
+
+        @pl.when(q + s <= nq - 1)
+        def _():
+            act(q + s, h)
+
+    @pl.loop(0, micro)
+    def _(m):
+        others(m, lambda r, h: key_out(r, h).start())
 
     loads[0].wait()
     loads[1].wait()
@@ -212,31 +216,17 @@
                 [turned[(r * nd + p) * share : (r * nd + p + 1) * share] for r in range(nq)], axis=0
             ).astype(BF16)
 
-    def others(m, act):
-        s, h = m // sub + 1, lax.rem(m, sub)
-
-        @pl.when(q - s >= 0)
-        def _():
-            act((q - s) * sub + h, True)
-
-        @pl.when(q + s <= nq - 1)
-        def _():
-            act((q + s) * sub + h, False)
-
-    def pass_on(k, upward):
-        key_up(k).wait_recv()
-        if upward:
-            @pl.when(q < nq - 1)
-            def _():
-                key_up(k).start()
-        else:
-            @pl.when(q > 0)
-            def _():
-                key_down(k).start()
+    loads[2].wait()
+    fold(q)
+
+    def pass_on(r, h):
+        k = r * sub + h
+        key_in(k).wait_recv()
         key_side(k).start()
         key_mate(k, 0, d).start()
 
-    def pass_side(k, upward):
+    def pass_side(r, h):
+        k = r * sub + h
         key_side_in(k).wait_recv()
         key_mate(k, 1, side).start()
 
@@ -264,13 +254,8 @@
         def _():
             others(m - 2, pass_side)
 
-        @pl.when(m == 0)
-        def _():
-            loads[2].wait()
-
         def both(i, carry):
-            r = jnp.where(m == 0, q, q + ((m - 3) // sub + 1) * (2 * i - 1))
-            own = (m == 0) & (i == 0)
+            r = q + ((m - 3) // sub + 1) * (2 * i - 1)
             later = (m >= 3) & (lax.rem(m, sub) == 2 % sub) & (r >= 0) & (r <= nq - 1)
 
             @pl.when(later)
@@ -278,9 +263,6 @@
                 for h in range(sub):
                     key_mate(r * sub + h, 0, mate).wait_recv()
                     key_mate(r * sub + h, 1, cross).wait_recv()
-
-            @pl.when(own | later)
-            def _():
                 fold(r)
 
             return carry
@@ -323,50 +305,42 @@
     def grad_side(k):
         return remote(x_out.at[k], x_in.at[k], gx_send.at[k], gx_recv.at[k], {"dp": side})
 
-    def grad_up(k):
-        return remote(z_out.at[k], up_in.at[k], gu_send.at[k], gu_recv.at[k], above)
-
-    def grad_down(k):
-        return remote(z_out.at[k], down_in.at[k], gd_send.at[k], gd_recv.at[k], below)
-
-    def in_turn(act_up, act_down, act_own):
-        def at(t, carry):
-            for_up = nq - 1 - (t - q)
-            for_down = t - (nq - 1 - q)
-
-            def half(h, carry):
-                @pl.when((t >= q) & (for_up > q))
-                def _():
-                    act_up(for_up * sub + h)
-
-                @pl.when((for_down >= 0) & (for_down < q))
-                def _():
-                    act_down(for_down * sub + h)
-
-                return carry
-
-            lax.fori_loop(0, sub, half, 0)
-            return carry
-
-        lax.fori_loop(0, nq - 1, at, 0)
-        for h in range(sub):
-            act_own(q * sub + h)
-
-    def start_mate(k):
-        grad_mate(k).start()
+    def grad_out(r, h):
+        return remote(
+            z_out.at[r * sub + h], z_in.at[q * sub + h], gu_send.at[r * sub + h],
+            gu_recv.at[q * sub + h], {"queue": r},
+        )
+
+    def grad_in(k):
+        return remote(z_out.at[k], z_in.at[k], gu_send.at[k], gu_recv.at[k], {"queue": k // sub})
+
+    def in_turn(act, own=True):
+        @pl.loop(0, micro)
+        def _(m):
+            back = (nq - 2 - m // sub) * sub + lax.rem(m, sub)
+            others(back, act)
+
+        if own:
+            @pl.loop(0, sub)
+            def _(h):
+                act(q, h)
+
+    def start_mate(r, h):
+        grad_mate(r * sub + h).start()
 
     term(cross, core_out)
-    in_turn(start_mate, start_mate, start_mate)
+    in_turn(start_mate)
     term(side, part)
     term(mate, keep_out)
     grad_keep().start()
 
-    def start_side(k):
+    def start_side(r, h):
+        k = r * sub + h
         grad_mate(k).wait_recv()
         x_out[k] = (part[k] + core_in[k].astype(F32)).astype(BF16)
         grad_side(k).start()
 
-    in_turn(start_side, start_side, start_side)
+    in_turn(start_side)
     fresh_move(0, side, side).wait_recv()
     fresh_move(2, side, mate).start()
     term(d, part)
@@ -413,82 +387,51 @@
 
     stores[1].start()
 
-    def up_step(k):
+    def send_on(r, h):
+        k = r * sub + h
         grad_side(k).wait_recv()
-        part[k] += x_in[k].astype(F32)
-
-        @pl.when(q > 0)
-        def _():
-            grad_up(k).wait_recv()
-            part[k] += up_in[k].astype(F32)
-
-        z_out[k] = part[k].astype(BF16)
-        grad_up(k).start()
-
-    def down_step(k):
-        grad_side(k).wait_recv()
-        part[k] += x_in[k].astype(F32)
-
-        @pl.when(q < nq - 1)
-        def _():
-            grad_down(k).wait_recv()
-            part[k] += down_in[k].astype(F32)
-
-        z_out[k] = part[k].astype(BF16)
-        grad_down(k).start()
+        z_out[k] = (part[k] + x_in[k].astype(F32)).astype(BF16)
+        grad_out(r, h).start()
 
     def own_out(h):
         return pltpu.make_async_copy(
             part.at[q * sub + h], grad_hbm.at[pl.ds(h * thin, thin)], store_sem.at[2 + h]
         )
 
-    def own_step(k):
-        grad_side(k).wait_recv()
-        part[k] += x_in[k].astype(F32)
-
-        @pl.when(q > 0)
-        def _():
-            grad_up(k).wait_recv()
-            part[k] += up_in[k].astype(F32)
-
-        @pl.when(q < nq - 1)
-        def _():
-            grad_down(k).wait_recv()
-            part[k] += down_in[k].astype(F32)
-
-    in_turn(up_step, down_step, lambda k: None)
+    in_turn(send_on, own=False)
+
+    def own_step(h):
+        mine = q * sub + h
+        grad_side(mine).wait_recv()
+        part[mine] += x_in[mine].astype(F32)
+
+        def add(r, carry):
+            @pl.when(r != q)
+            def _():
+                grad_in(r * sub + h).wait_recv()
+                part[mine] += z_in[r * sub + h].astype(F32)
+
+            return carry
+
+        lax.fori_loop(0, nq, add, 0)
+        own_out(h).start()
+
     for h in range(sub):
-        own_step(q * sub + h)
-        own_out(h).start()
+        own_step(h)
 
     def drain(k, carry):
         r = k // sub
 
-        @pl.when((r <= q) & (q < nq - 1))
-        def _():
-            key_up(k).wait_send()
-
-        @pl.when((r >= q) & (q > 0))
-        def _():
-            key_down(k).wait_send()
-
         @pl.when(r != q)
         def _():
+            key_out(r, lax.rem(k, sub)).wait_send()
             key_side(k).wait_send()
             key_mate(k, 0, d).wait_send()
             key_mate(k, 1, side).wait_send()
+            grad_out(r, lax.rem(k, sub)).wait_send()
 
         grad_mate(k).wait_send()
         grad_side(k).wait_send()
-
-        @pl.when(r > q)
-        def _():
-            grad_up(k).wait_send()
-
-        @pl.when(r < q)
-        def _():
-            grad_down(k).wait_send()
-
         return carry
 
     lax.fori_loop(0, blocks, drain, 0)
@@ -575,10 +518,9 @@
                 V((blocks, thin, width), BF16),
                 V((blocks, thin, width), BF16),
                 V((blocks, thin, width), BF16),
-                V((blocks, thin, width), BF16),
-                S((8,)), S((2 + sub,)), each, each, each, each, each, S((blocks, 2)), S((blocks, 2)),
+                S((8,)), S((2 + sub,)), each, each, each, each, S((blocks, 2)), S((blocks, 2)),
                 S((nq,)), S((nq,)), S((3,)), S((3,)),
-                each, each, S((1,)), S((1,)), each, each, each, each, each, each,
+                each, each, S((1,)), S((1,)), each, each, each, each,
             ],
             compiler_params=pltpu.CompilerParams(
                 collective_id=0, has_side_effects=True, vmem_limit_bytes=56 * 2**20

time: 50.5 us -> 49.7 us (0.984)
  Pallas kernels: 49.1 us -> 48.3 us
    pallas_call x1, Pallas kernels: 47 us -> 46.2 us  [body(): pl.pallas_call(functools.partial(kernel, nq, nd), out_shape=outs, in_spec...]
where the time goes in v4:
time: 49.7 us; the launch traced here: 49.6 us
  Pallas kernels  48.3 us (97%)
  between operations  1.29 us (3%)
    pallas_call x1, Pallas kernels, body(): pl.pallas_call(functools.partial(kernel, nq, nd), out_shape=outs, in_spec...  46.2 us
    pallas_call x1, Pallas kernels, body(): pl.pallas_call(finish, out_shape=outs, in_specs=[vmem] * 3, out_specs=(vm...  2.03 us

profile of v4, /device:TPU:0, one launch (start us, length us, event | category | flops | bytes accessed | tf_op | source)
XLA Modules:
  0.0 49.6 jit_solution(6476061983496536265)
XLA Ops:
  1.3 46.2 %contrast.1 = (f32[1,256]{1,0:T(1,128)}, f32[64,1024]{1,0:T(8,128)}, bf16[256,1024]{1,0:T(8,128)(2,1)}) custom-call(s32[1]{0:T(128)S(6)} %copy.11.pointer_hbm, s32[16]{0:T(128)} %owner_hbm.1, s32[1,256]{1,0:T(1,128)} %bitcast.2, bf16[256,1024]{1,0:T(8,128)(2,1)} %x_hbm.1, bf16[16,1024]{1,0:T(8,128)(2,1)} %kin_hbm.1, bf16[1024,1024]{1,0:T(8,128)(2,1)} %wq_hbm.1, ...), custom_call_target="tpu_custom_call" | custom-call | tf_op jit(solution)/shard_map/contrast/pallas_call | solution.py:480
  47.5 2.0 %finish.1 = (f32[1,256]{1,0:T(1,128)}, f32[64,1024]{1,0:T(8,128)}, bf16[256,1024]{1,0:T(8,128)(2,1)}) custom-call(f32[1,256]{1,0:T(1,128)} %get-tuple-element.9.loss_in, f32[64,1024]{1,0:T(8,128)} %get-tuple-element.10.grad_in, bf16[256,1024]{1,0:T(8,128)(2,1)} %get-tuple-element.11.queue_in), custom_call_target="tpu_custom_call" | custom-call | tf_op jit(solution)/shard_map/finish/pallas_call | solution.py:533

commit v5 on v2

--- a/solution.py
+++ b/solution.py
@@ -9,7 +9,6 @@
 
 temper = 0.05
 splits = 2
-cuts = 4
 MESH = pl.DeviceIdType.MESH
 F32 = jnp.float32
 BF16 = jnp.bfloat16
@@ -179,9 +178,6 @@
                 [turned[(r * nd + p) * share : (r * nd + p + 1) * share] for r in range(nq)], axis=0
             ).astype(BF16)
 
-    loads[2].wait()
-    fold(q)
-
     def others(m, act):
         s, h = m // sub + 1, lax.rem(m, sub)
 
@@ -215,14 +211,6 @@
         def _():
             others(m, pass_on)
 
-        @pl.when(m == 0)
-        def _():
-            make_fresh()
-
-        @pl.when(m == 1)
-        def _():
-            turn()
-
         @pl.when(m == micro - 1)
         def _():
             for r in range(nq):
@@ -233,6 +221,19 @@
         @pl.when((m >= 2) & (m < micro + 2))
         def _():
             others(m - 2, pass_side)
+
+        @pl.when(m == 1)
+        def _():
+            loads[2].wait()
+            fold(q)
+
+        @pl.when(m == 2)
+        def _():
+            make_fresh()
+
+        @pl.when(m == 3)
+        def _():
+            turn()
 
         @pl.when((m >= 3) & (lax.rem(m, sub) == (sub + 2) % sub))
         def _():
@@ -446,17 +447,10 @@
         own_out(h).wait()
 
 
-def finish(cuts, loss_in, grad_in, queue_in, loss_out, grad_out, queue_out, sem):
-    copies = [pltpu.make_async_copy(loss_in, loss_out, sem.at[0])]
-    for src, dst in ((grad_in, grad_out), (queue_in, queue_out)):
-        n = src.shape[0] // cuts if src.shape[0] % (16 * cuts) == 0 else src.shape[0]
-        for at in range(0, src.shape[0], n):
-            piece = pl.ds(at, n)
-            copies.append(pltpu.make_async_copy(src.at[piece], dst.at[piece], sem.at[len(copies)]))
-    for copy in copies:
-        copy.start()
-    for copy in copies:
-        copy.wait()
+def finish(loss_in, grad_in, queue_in, loss_out, grad_out, queue_out):
+    loss_out[...] = loss_in[...]
+    grad_out[...] = grad_in[...]
+    queue_out[...] = queue_in[...]
 
 
 def make_body(nq, nd):
@@ -471,6 +465,7 @@
         share = width // (nq * nd)
         sub = splits if share % (16 * splits) == 0 else 1
         blocks, thin = nq * sub, share // sub
+        vmem = pl.BlockSpec(memory_space=pltpu.VMEM)
         hbm = pl.BlockSpec(memory_space=pl.ANY)
         V = pltpu.VMEM
         S = pltpu.SemaphoreType.DMA
@@ -531,11 +526,10 @@
             query_inputs, key_inputs, query_weight, key_weight, queue_keys,
         )
         loss, grad, queue = pl.pallas_call(
-            functools.partial(finish, cuts),
+            finish,
             out_shape=outs,
-            in_specs=[hbm] * 3,
-            out_specs=(hbm,) * 3,
-            scratch_shapes=[S((1 + 2 * cuts,))],
+            in_specs=[vmem] * 3,
+            out_specs=(vmem,) * 3,
             name="finish",
         )(*made)
         return loss.reshape(rows), grad, queue

time: 71.1 us -> 48.7 us (0.68)
  Pallas kernels: 69.7 us -> 47.3 us
    pallas_call x1, Pallas kernels: 25 us -> 2.03 us  [body(): pl.pallas_call(finish, out_shape=outs, in_specs=[vmem] * 3, out_specs=(vm...]
where the time goes in v5:
time: 48.7 us; the launch traced here: 48.6 us
  Pallas kernels  47.3 us (97%)
  between operations  1.29 us (3%)
    pallas_call x1, Pallas kernels, body(): pl.pallas_call(functools.partial(kernel, nq, nd), out_shape=outs, in_spec...  45.3 us
    pallas_call x1, Pallas kernels, body(): pl.pallas_call(finish, out_shape=outs, in_specs=[vmem] * 3, out_specs=(vm...  2.03 us

profile of v5, /device:TPU:0, one launch (start us, length us, event | category | flops | bytes accessed | tf_op | source)
XLA Modules:
  0.0 48.6 jit_solution(7807576754605010295)
XLA Ops:
  1.3 45.3 %contrast.1 = (f32[1,256]{1,0:T(1,128)}, f32[64,1024]{1,0:T(8,128)}, bf16[256,1024]{1,0:T(8,128)(2,1)}) custom-call(s32[1]{0:T(128)S(6)} %copy.11.pointer_hbm, s32[16]{0:T(128)} %owner_hbm.1, s32[1,256]{1,0:T(1,128)} %bitcast.2, bf16[256,1024]{1,0:T(8,128)(2,1)} %x_hbm.1, bf16[16,1024]{1,0:T(8,128)(2,1)} %kin_hbm.1, bf16[1024,1024]{1,0:T(8,128)(2,1)} %wq_hbm.1, ...), custom_call_target="tpu_custom_call" | custom-call | tf_op jit(solution)/shard_map/contrast/pallas_call | solution.py:478
  46.5 2.0 %finish.1 = (f32[1,256]{1,0:T(1,128)}, f32[64,1024]{1,0:T(8,128)}, bf16[256,1024]{1,0:T(8,128)(2,1)}) custom-call(f32[1,256]{1,0:T(1,128)} %get-tuple-element.9.loss_in, f32[64,1024]{1,0:T(8,128)} %get-tuple-element.10.grad_in, bf16[256,1024]{1,0:T(8,128)(2,1)} %get-tuple-element.11.queue_in), custom_call_target="tpu_custom_call" | custom-call | tf_op jit(solution)/shard_map/finish/pallas_call | solution.py:528
